TPU v7x, 32 devices: a whole 2x2x4 slice. The times are simulated.
32 devices in a mesh: grp: 2 (over y), path: 4 (over z), scen: 2 (over x), sub: 2 (over core).
Axes of the slice: x: 2, y: 2, z: 4, core: 2. Of those that a mesh axis runs over, the one named last changes fastest.
Arguments:
- path_links: int32 [8, 16384], P(None, ('grp', 'path')), parts along dimension 1, may hold values from -1 to 3583, as said below
- block_tiles: int32 [128, 16], P(('grp', 'path')), parts along dimension 0, may hold values from 0 to 27, as said below
- block_count: int32 [128], P(('grp', 'path')), parts along dimension 0, may hold values from 1 to 16
- path_commodity: int32 [128, 128], P(('grp', 'path')), parts along dimension 0, may hold values from 0 to 31, never falling along the last dimension, each value on 1 to 8 neighbouring positions
- demand: int32 [256, 4096], P(('scen', 'sub'), ('grp', 'path')), parts along dimension 1, may hold values from 1 to 64
- lengths: float32 [256, 7168], P(('scen', 'sub'), ('grp', 'path')), parts along dimension 1, may hold values from 0.05 to 10
- capacity: float32 [7168], P(('grp', 'path')), parts along dimension 0, may hold values from 4 to 32
- scenario_weight: float32 [512], P(('grp', 'scen', 'sub')), parts along dimension 0, may hold values from 0.5 to 2
Outputs:
- flows: float32 [256, 16384], P(('scen', 'sub'), ('grp', 'path')), parts along dimension 1
- lengths_next: float32 [256, 7168], P(('scen', 'sub'), ('grp', 'path')), parts along dimension 1
- robust_cost: float32 [16384], P(('grp', 'path')), parts along dimension 0
There are 2 independent parts, one for each index of `grp`. A program takes and returns all parts, laid end to end along the dimension named above; each array names one. Nothing has to cross between parts.
Inputs may be any that keep to these rules, and one draw needn't show every extreme that they name: `path_links`: entry [h, p] is the link of hop h of path p, or -1 past the path's last hop (hop 0 is never -1). Every link of a path in block b = p // 128 lies in a link block named by block_tiles[b, 0] to block_tiles[b, block_count[b] - 1]; link block j holds links j * 128 to (j + 1) * 128 - 1. `block_tiles`: the entries of one row are distinct link blocks.
All inputs are finite; a program needn't handle non-finite values.
Results may differ from a plain program's by a relative error of at most 0.0003.
Values sent between devices are 32-bit elements; how exact they have to be, the bound alone decides.
No kernel may reach another device: no remote copies, remote signals or barrier semaphores. Data moves between devices by JAX's collectives and lax.ppermute only.
A program may use at most 64 MiB of HBM per device.

v0:
```python
import jax
import jax.numpy as jnp
from jax import lax
from jax.sharding import PartitionSpec as P

PATHS_PER_BLOCK = 128
LB = 128
MAXT = 16
COMMODITY_BLOCK = 32
S = 256
SOFTMIN_RATE = 0.25
STEP_RATE = 1.0
DEMAND_UNIT = 0.0625
PRECISE = lax.Precision.HIGHEST


def incidence(hop_links, tile_ids, live_count):
    link_block = hop_links // LB
    column = hop_links % LB
    live_slots = jnp.arange(MAXT) < live_count
    slot_match = (
        (link_block[:, :, None] == tile_ids[None, None, :]) & live_slots[None, None, :]
    ).astype(jnp.float32)
    column_hot = (column[:, :, None] == jnp.arange(LB)[None, None, :]).astype(jnp.float32)
    return jnp.einsum("hpt,hpl->ptl", slot_match, column_hot, precision=PRECISE)


def tile_costs(table_grid, tile_ids, tile_hits):
    chosen = jnp.take(table_grid, tile_ids, axis=1)
    return jnp.einsum("stl,ptl->sp", chosen, tile_hits, precision=PRECISE)


def tile_loads(block_flow, tile_hits):
    return jnp.einsum("sp,ptl->stl", block_flow, tile_hits, precision=PRECISE)


def block_flows(block_cost, commodity_id, block_demand):
    commodity_onehot = (commodity_id[:, None] == jnp.arange(COMMODITY_BLOCK)[None, :]).astype(
        jnp.float32
    )
    weight = jnp.exp(-SOFTMIN_RATE * block_cost)
    totals = jnp.dot(
        weight, commodity_onehot, preferred_element_type=jnp.float32, precision=PRECISE
    )
    per_path = jnp.dot(
        totals, commodity_onehot.T, preferred_element_type=jnp.float32, precision=PRECISE
    )
    wanted = jnp.dot(
        block_demand.astype(jnp.float32) * DEMAND_UNIT,
        commodity_onehot.T,
        preferred_element_type=jnp.float32,
        precision=PRECISE,
    )
    return wanted * weight / per_path


def flow_sweep(length_wide, links_by_block, tile_table, count_table, comm_table, block_demands):
    scenario_rows = length_wide.shape[0]
    length_grid = length_wide.reshape(scenario_rows, -1, LB)

    def first_pass(load_grid, pieces):
        hop_links, tile_ids, live_count, commodity_id, block_demand = pieces
        tile_hits = incidence(hop_links, tile_ids, live_count)
        block_cost = tile_costs(length_grid, tile_ids, tile_hits)
        block_flow = block_flows(block_cost, commodity_id, block_demand)
        load_grid = load_grid.at[:, tile_ids, :].add(tile_loads(block_flow, tile_hits))
        return (load_grid, block_flow)

    load_grid, flow_blocks = lax.scan(
        first_pass,
        jnp.zeros(length_grid.shape, jnp.float32),
        (links_by_block, tile_table, count_table, comm_table, block_demands),
    )
    flows = flow_blocks.transpose(1, 0, 2).reshape(scenario_rows, -1)
    return (flows, load_grid.reshape(scenario_rows, -1))


def cost_sweep(next_wide, weight_rows, links_by_block, tile_table, count_table):
    scenario_rows = next_wide.shape[0]
    next_grid = next_wide.reshape(scenario_rows, -1, LB)

    def second_pass(carried, pieces):
        hop_links, tile_ids, live_count = pieces
        tile_hits = incidence(hop_links, tile_ids, live_count)
        block_cost = tile_costs(next_grid, tile_ids, tile_hits)
        mixed = (
            jnp.dot(
                weight_rows[None, :],
                block_cost,
                preferred_element_type=jnp.float32,
                precision=PRECISE,
            )[0]
            / S
        )
        return (carried, mixed)

    _, partial_value = lax.scan(
        second_pass, jnp.zeros((), jnp.float32), (links_by_block, tile_table, count_table)
    )
    return partial_value.reshape(-1)


def body(
    path_links, block_tiles, block_count, path_commodity, demand, lengths, capacity, scenario_weight
):
    hop_count, path_total = path_links.shape
    block_list = block_tiles.shape[0]
    scenario_rows, link_rows = lengths.shape
    links_by_block = path_links.reshape(hop_count, block_list, PATHS_PER_BLOCK).transpose(1, 0, 2)
    block_demands = demand.reshape(scenario_rows, block_list, COMMODITY_BLOCK).transpose(1, 0, 2)
    gathered = lax.all_gather(lengths, "path", axis=1, tiled=True)
    flows, load_full = flow_sweep(
        gathered, links_by_block, block_tiles, block_count, path_commodity, block_demands
    )
    link_total = gathered.shape[1]
    own_loads = lax.psum_scatter(load_full, "path", scatter_dimension=1, tiled=True)
    grown_len = lengths * jnp.exp(STEP_RATE * own_loads / capacity[None, :])
    totals = lax.psum(jnp.sum(grown_len, axis=1), "path")
    lengths_next = grown_len * (link_total / totals)[:, None]
    wide_next = lax.all_gather(lengths_next, "path", axis=1, tiled=True)
    partial_value = cost_sweep(wide_next, scenario_weight, links_by_block, block_tiles, block_count)
    robust = lax.psum(partial_value, ("scen", "sub"))
    return (flows, lengths_next, robust)


def solution(mesh):
    return jax.shard_map(
        body,
        mesh=mesh,
        in_specs=(
            P(None, ("grp", "path")),
            P(("grp", "path"), None),
            P(("grp", "path")),
            P(("grp", "path"), None),
            P(("scen", "sub"), ("grp", "path")),
            P(("scen", "sub"), ("grp", "path")),
            P(("grp", "path")),
            P(("grp", "scen", "sub")),
        ),
        out_specs=(
            P(("scen", "sub"), ("grp", "path")),
            P(("scen", "sub"), ("grp", "path")),
            P(("grp", "path")),
        ),
        check_vma=False,
    )
```

profile of v0, /device:TPU:0, one launch (start us, length us, event | category | flops | bytes accessed | tf_op | source)
XLA Modules:
  0.0 389.9 jit_solution(973819889943569372)
XLA Ops:
  7.2 23.0 %all_gather.6 = f32[64,3584]{1,0:T(8,128)S(1)} all-gather(f32[64,896]{1,0:T(8,128)} %param.19), channel_id=1, replica_groups=mesh['grp'=2,'path'=4,'scen'=2,'sub'=2] {'path'}, dimensions={1}, use_global_device_ids=true | all-gather | bytes 1146880 | tf_op jit(solution)/shard_map/all_gather | solution.py:111
  32.6 185.0 %while.26 = (s32[]{:T(128)}, f32[64,28,128]{2,0,1:T(8,128)S(1)}, f32[16,64,128]{2,1,0:T(8,128)}, s32[16,16]{1,0:T(8,128)}, s32[16,64,32]{1,2,0:T(8,128)}, /*inde...) while((s32[]{:T(128)}, f32[64,28,128]{2,0,1:T(8,128)S(1)}, ...), condition=%wide.region_2.4_spmd, body=%wide.region_0.3_spmd.sunk | while | flops 416772288 | bytes 7180105 | solution.py:69
  36.8 1.4 fusion.88
  48.3 1.4 fusion.88
  59.9 1.4 fusion.88
  71.5 1.4 fusion.88
  83.0 1.4 fusion.88
  94.6 1.4 fusion.88
  106.2 1.4 fusion.88
  117.7 1.4 fusion.88
  129.3 1.4 fusion.88
  140.9 1.4 fusion.88
  152.4 1.4 fusion.88
  164.0 1.4 fusion.88
  175.6 1.4 fusion.88
  187.1 1.4 fusion.88
  198.7 1.4 fusion.88
  210.3 1.4 fusion.88
  220.5 23.0 %reduce-scatter.2.cloned.1.call-done = f32[64,896]{1,0:T(8,128)} async-done(((f32[64,3584]{1,0:T(8,128)}), f32[64,896]{1,0:T(8,128)}) %reduce-scatter.2.cloned.1.call-update) | async-done | bytes 229392 | tf_op jit(solution)/shard_map/reduce_scatter | solution.py:116
  244.6 9.7 %psum.14 = f32[64]{0:T(128)S(1)} all-reduce(f32[64]{0:T(128)S(1)} %fusion.47), channel_id=1, replica_groups=mesh['grp'=2,'path'=4,'scen'=2,'sub'=2] {'path'}, use_global_device_ids=true, to_apply=%region_5.7 | all-reduce | flops 64 | bytes 512 | tf_op jit(solution)/shard_map/psum | solution.py:118
  254.5 18.4 %all_gather.7 = f32[64,3584]{1,0:T(8,128)S(1)} all-gather(f32[64,896]{1,0:T(8,128)S(1)} %broadcast_multiply_fusion), channel_id=1, replica_groups=mesh['grp'=2,'path'=4,'scen'=2,'sub'=2] {'path'}, dimensions={1}, use_global_device_ids=true | all-gather | bytes 1146880 | tf_op jit(solution)/shard_map/all_gather | solution.py:120
  273.5 103.2 %while.27 = (s32[]{:T(128)}, f32[16,128]{1,0:T(8,128)S(1)}, s32[16,16]{1,0:T(8,128)}, f32[64,28,128]{2,0,1:T(8,128)S(1)}, s32[16,8,128]{2,1,0:T(8,128)}, /*index...) while((s32[]{:T(128)}, f32[16,128]{1,0:T(8,128)S(1)}, s32[16,16]{1,0:T(8,128)}, ...), condition=%wide.region_7.9_spmd, body=%wide.region_6.8_spmd.sunk | while | flops 205941024 | bytes 4063613 | solution.py:97
  278.4 1.4 convolution_bitcast_fusion.7
  284.8 1.4 convolution_bitcast_fusion.7
  291.3 1.4 convolution_bitcast_fusion.7
  297.7 1.4 convolution_bitcast_fusion.7
  304.2 1.4 convolution_bitcast_fusion.7
  310.6 1.4 convolution_bitcast_fusion.7
  317.1 1.4 convolution_bitcast_fusion.7
  323.5 1.4 convolution_bitcast_fusion.7
  330.0 1.4 convolution_bitcast_fusion.7
  376.7 6.3 %psum.15 = f32[2048]{0:T(1024)} all-reduce(f32[2048]{0:T(1024)S(1)} %bitcast.175), channel_id=1, replica_groups=mesh['grp'=2,'path'=4,'scen'=2,'sub'=2] {'scen','sub'}, use_global_device_ids=true, to_apply=%region_8.10 | all-reduce | flops 2048 | bytes 16384 | tf_op jit(solution)/shard_map/psum | solution.py:122
  (516 shorter events, 258.5 us)
Async XLA Ops:
  7.2 236.3 %reduce-scatter.2.cloned.1.call-start = ((), (), s32[]{:S(2)}) async-start(), calls=%async_computation.1 | async-start | bytes 1146880 | tf_op jit(solution)/shard_map/reduce_scatter | solution.py:116
  30.2 0.9 copy-start.4
  31.9 0.7 copy-start.7
  218.6 1.0 copy-start.3
  219.7 23.8 %copy-start = (f32[64,896]{1,0:T(8,128)S(1)}, f32[64,896]{1,0:T(8,128)}, u32[]{:S(2)}) copy-start(f32[64,896]{1,0:T(8,128)} %param.19) | copy-start | bytes 688132
  219.7 23.8 %copy-start.5 = (f32[896]{0:T(1024)S(1)}, f32[896]{0:T(1024)}, u32[]{:S(2)}) copy-start(f32[896]{0:T(1024)} %param.20) | copy-start | bytes 10756
  243.5 10.9 %copy-start.1 = (f32[64,896]{1,0:T(8,128)S(1)}, f32[64,896]{1,0:T(8,128)}, u32[]{:S(2)}) copy-start(f32[64,896]{1,0:T(8,128)} %reduce-scatter.2.cloned.1.call-done) | copy-start | bytes 688132
  254.4 18.4 %copy-start.2 = (f32[64,896]{1,0:T(8,128)}, f32[64,896]{1,0:T(8,128)S(1)}, u32[]{:S(2)}) copy-start(f32[64,896]{1,0:T(8,128)S(1)} %broadcast_multiply_fusion) | copy-start | bytes 688132
  272.8 0.7 copy-start.6
Sparse Core Ops, SparseCore 0:
  218.8 24.6 reduce-scatter.1
where the time goes:
time: 395 us; the launch traced here: 390 us
  other arithmetic  106 us (27%)
  matrix products  106 us (27%)
  local copies, waits for them, and re-layouts  80.8 us (20%)
  blocking collectives  57.4 us (15%)
  waiting for transfers between devices  23 us (6%)
  between operations  14.1 us (4%)
    dynamic_slice x96, local copies, waits for them, and re-layouts, flow_sweep(): lax.scan(first_pass, jnp.zeros(length_grid.shape, jnp.float32), (links_by...  44.7 us
    dot_general x32, matrix products, tile_costs(): return jnp.einsum('stl,ptl->sp', chosen, tile_hits, precision=PRECISE)  44.3 us
    and x32, other arithmetic, tile_costs(): chosen = jnp.take(table_grid, tile_ids, axis=1)  42.4 us
    reduce_scatter x1, waiting for transfers between devices, body(): lax.psum_scatter(load_full, 'path', scatter_dimension=1, tiled=True)  23 us
    all_gather x1, blocking collectives, body(): gathered = lax.all_gather(lengths, 'path', axis=1, tiled=True)  23 us
    scatter-add x16, other arithmetic, first_pass(): load_grid.at[:, tile_ids, :].add(tile_loads(block_flow, tile_hits))  21.2 us
    dot_general x32, matrix products, incidence(): return jnp.einsum('hpt,hpl->ptl', slot_match, column_hot, precision=PRECISE)  21.2 us
    gather x32, local copies, waits for them, and re-layouts, tile_costs(): chosen = jnp.take(table_grid, tile_ids, axis=1)  18.6 us
  transfers between devices with their start and end apart: 1, of which 1 were waited for; matrix products, arithmetic and copies ran while one was open for 0% of the time, Pallas kernels for 0%

commit v1 on v0

--- a/solution.py
+++ b/solution.py
@@ -115,7 +115,7 @@
     link_total = gathered.shape[1]
     own_loads = lax.psum_scatter(load_full, "path", scatter_dimension=1, tiled=True)
     grown_len = lengths * jnp.exp(STEP_RATE * own_loads / capacity[None, :])
-    totals = lax.psum(jnp.sum(grown_len, axis=1), "path")
+    totals = jnp.sum(lax.all_gather(jnp.sum(grown_len, axis=1), "path"), axis=0)
     lengths_next = grown_len * (link_total / totals)[:, None]
     wide_next = lax.all_gather(lengths_next, "path", axis=1, tiled=True)
     partial_value = cost_sweep(wide_next, scenario_weight, links_by_block, block_tiles, block_count)

time: 395 us -> 418 us (1.058)
  other arithmetic: 106 us -> 133 us
  local copies, waits for them, and re-layouts: 80.8 us -> 70.5 us
  matrix products: 106 us -> 111 us
    select_n x16 -> x32, other arithmetic: 11.2 us -> 28.1 us  [incidence(): column = hop_links % LB]
    select_n x32, other arithmetic: 12.1 us -> 28.4 us  [incidence(): link_block = hop_links // LB]
    dynamic_slice x96 -> x64, local copies, waits for them, and re-layouts: 44.7 us -> 31.6 us  [flow_sweep(): lax.scan(first_pass, jnp.zeros(length_grid.shape, jnp.float32), (links_by...]
    psum x1 -> x0, blocking collectives: 9.72 us -> none  [body(): totals = lax.psum(jnp.sum(grown_len, axis=1), 'path')]
    unnamed x0 -> x1, blocking collectives: none -> 9.68 us
    dot_general x32, matrix products: 21.2 us -> 25.8 us  [incidence(): return jnp.einsum('hpt,hpl->ptl', slot_match, column_hot, precision=PRECISE)]
where the time goes in v1:
time: 418 us; the launch traced here: 411 us
  other arithmetic  133 us (32%)
  matrix products  111 us (27%)
  local copies, waits for them, and re-layouts  70.5 us (17%)
  blocking collectives  57.1 us (14%)
  waiting for transfers between devices  22 us (5%)
  between operations  14.8 us (4%)
    dot_general x32, matrix products, tile_costs(): return jnp.einsum('stl,ptl->sp', chosen, tile_hits, precision=PRECISE)  44.4 us
    and x32, other arithmetic, tile_costs(): chosen = jnp.take(table_grid, tile_ids, axis=1)  43 us
    dynamic_slice x64, local copies, waits for them, and re-layouts, flow_sweep(): lax.scan(first_pass, jnp.zeros(length_grid.shape, jnp.float32), (links_by...  31.6 us
    select_n x32, other arithmetic, incidence(): link_block = hop_links // LB  28.4 us
    select_n x32, other arithmetic, incidence(): column = hop_links % LB  28.1 us
    dot_general x32, matrix products, incidence(): return jnp.einsum('hpt,hpl->ptl', slot_match, column_hot, precision=PRECISE)  25.8 us
    all_gather x1, blocking collectives, body(): gathered = lax.all_gather(lengths, 'path', axis=1, tiled=True)  22.7 us
    reduce_scatter x1, waiting for transfers between devices, body(): lax.psum_scatter(load_full, 'path', scatter_dimension=1, tiled=True)  22 us
  transfers between devices with their start and end apart: 1, of which 1 were waited for; matrix products, arithmetic and copies ran while one was open for 0% of the time, Pallas kernels for 0%

profile of v1, /device:TPU:0, one launch (start us, length us, event | category | flops | bytes accessed | tf_op | source)
XLA Modules:
  0.0 411.4 jit_solution(376771118940815321)
XLA Ops:
  7.2 2.2 copy.30
  9.4 22.7 %all_gather.12 = f32[64,3584]{1,0:T(8,128)S(1)} all-gather(f32[64,896]{1,0:T(8,128)S(1)} %copy-done), channel_id=1, replica_groups=mesh['grp'=2,'path'=4,'scen'=2,'sub'=2] {'path'}, dimensions={1}, use_global_device_ids=true | all-gather | bytes 1146880 | tf_op jit(solution)/shard_map/all_gather | solution.py:111
  34.6 200.3 %while.26 = (s32[]{:T(128)}, f32[64,28,128]{2,0,1:T(8,128)S(1)}, f32[16,64,128]{2,1,0:T(8,128)}, s32[16,16]{1,0:T(8,128)}, s32[16,64,32]{1,2,0:T(8,128)}, /*inde...) while((s32[]{:T(128)}, f32[64,28,128]{2,0,1:T(8,128)S(1)}, ...), condition=%wide.region_2.4_spmd, body=%wide.region_0.3_spmd.sunk | while | flops 416778432 | bytes 7169869 | solution.py:69
  39.7 1.4 fusion.90
  52.2 1.4 fusion.90
  64.7 1.4 fusion.90
  77.2 1.4 fusion.90
  89.8 1.4 fusion.90
  102.3 1.4 fusion.90
  114.8 1.4 fusion.90
  127.3 1.4 fusion.90
  139.8 1.4 fusion.90
  152.3 1.4 fusion.90
  164.9 1.4 fusion.90
  177.4 1.4 fusion.90
  189.9 1.4 fusion.90
  202.4 1.4 fusion.90
  214.9 1.4 fusion.90
  227.4 1.4 fusion.90
  238.7 22.0 %reduce-scatter.2.cloned.1.call-done = f32[64,896]{1,0:T(8,128)} async-done(((f32[64,3584]{1,0:T(8,128)}), f32[64,896]{1,0:T(8,128)}) %reduce-scatter.2.cloned.1.call-update) | async-done | bytes 229392 | tf_op jit(solution)/shard_map/reduce_scatter | solution.py:116
  262.2 9.7 %all-reduce = f32[256]{0:T(256)S(1)} all-reduce(f32[256]{0:T(256)S(1)} %dynamic-update-slice), channel_id=2, replica_groups=mesh['grp'=2,'path'=4,'scen'=2,'sub'=2] {'path'}, use_global_device_ids=true, to_apply=%add | all-reduce | flops 256 | bytes 2048
  272.1 18.4 %all_gather.15 = f32[64,3584]{1,0:T(8,128)S(1)} all-gather(f32[64,896]{1,0:T(8,128)S(1)} %broadcast_multiply_fusion), channel_id=1, replica_groups=mesh['grp'=2,'path'=4,'scen'=2,'sub'=2] {'path'}, dimensions={1}, use_global_device_ids=true | all-gather | bytes 1146880 | tf_op jit(solution)/shard_map/all_gather | solution.py:120
  291.1 107.1 %while.27 = (s32[]{:T(128)}, f32[16,128]{1,0:T(8,128)S(1)}, s32[16,16]{1,0:T(8,128)}, f32[64,28,128]{2,0,1:T(8,128)S(1)}, s32[16,8,128]{1,2,0:T(8,128)}, /*index...) while((s32[]{:T(128)}, f32[16,128]{1,0:T(8,128)S(1)}, s32[16,16]{1,0:T(8,128)}, ...), condition=%wide.region_7.9_spmd, body=%wide.region_6.8_spmd.sunk | while | flops 205941024 | bytes 3768701 | solution.py:97
  302.9 1.4 convolution_bitcast_fusion.7
  309.6 1.4 convolution_bitcast_fusion.7
  323.0 1.4 convolution_bitcast_fusion.7
  343.1 1.4 convolution_bitcast_fusion.7
  349.8 1.4 convolution_bitcast_fusion.7
  363.2 1.4 convolution_bitcast_fusion.7
  383.3 1.4 convolution_bitcast_fusion.7
  390.0 1.4 convolution_bitcast_fusion.7
  398.2 6.3 %psum.7 = f32[2048]{0:T(1024)} all-reduce(f32[2048]{0:T(1024)S(1)} %bitcast.174), channel_id=1, replica_groups=mesh['grp'=2,'path'=4,'scen'=2,'sub'=2] {'scen','sub'}, use_global_device_ids=true, to_apply=%region_8.10 | all-reduce | flops 2048 | bytes 16384 | tf_op jit(solution)/shard_map/psum | solution.py:122
  (478 shorter events, 280.0 us)
Async XLA Ops:
  7.2 253.6 %reduce-scatter.2.cloned.1.call-start = ((), (), s32[]{:S(2)}) async-start(), calls=%async_computation.1 | async-start | bytes 1146880 | tf_op jit(solution)/shard_map/reduce_scatter | solution.py:116
  7.2 2.2 copy-start
  32.2 0.9 copy-start.5
  33.9 0.7 copy-start.8
  235.9 2.0 copy-start.4
  235.9 0.7 copy-start.9
  237.9 22.8 %copy-start.1 = (f32[64,896]{1,0:T(8,128)S(1)}, f32[64,896]{1,0:T(8,128)}, u32[]{:S(2)}) copy-start(f32[64,896]{1,0:T(8,128)} %param.19) | copy-start | bytes 688132
  237.9 22.8 %copy-start.6 = (f32[896]{0:T(1024)S(1)}, f32[896]{0:T(1024)}, u32[]{:S(2)}) copy-start(f32[896]{0:T(1024)} %param.20) | copy-start | bytes 10756
  260.7 11.2 %copy-start.2 = (f32[64,896]{1,0:T(8,128)S(1)}, f32[64,896]{1,0:T(8,128)}, u32[]{:S(2)}) copy-start(f32[64,896]{1,0:T(8,128)} %reduce-scatter.2.cloned.1.call-done) | copy-start | bytes 688132
  272.1 18.4 %copy-start.3 = (f32[64,896]{1,0:T(8,128)}, f32[64,896]{1,0:T(8,128)S(1)}, u32[]{:S(2)}) copy-start(f32[64,896]{1,0:T(8,128)S(1)} %broadcast_multiply_fusion) | copy-start | bytes 688132
  290.4 0.7 copy-start.7
Sparse Core Ops, SparseCore 0:
  236.0 24.6 reduce-scatter.1
